TPU v7x, 32 devices: a whole 2x2x4 slice. The times are simulated.
32 devices in a mesh: dp: 8 (over z, y), ctx: 4 (over x, core).
Axes of the slice: x: 2, y: 2, z: 4, core: 2. Of those that a mesh axis runs over, the one named last changes fastest.
Arguments:
- query_rows: bfloat16 [8192, 8192], P(('dp', 'ctx')), may hold values from -34 to 34
- key_rows: bfloat16 [8192, 1024], P(('dp', 'ctx')), may hold values from -10 to 10, as said below
- value_rows: bfloat16 [8192, 1024], P(('dp', 'ctx')), may hold values from -6 to 6
- grad_out: bfloat16 [8192, 8192], P(('dp', 'ctx')), may hold values from -6 to 6
- dest_rows: int32 [8192], P(('dp', 'ctx')), may hold values from 0 to 8191, as said below
- key_blocks: int32 [8, 8, 4], P('dp', 'ctx'), may hold values from 0 to 7, as said below
- key_count: int32 [8, 8], P('dp', 'ctx'), may hold values from 1 to 4, as said below
Outputs:
- attn_out: bfloat16 [8192, 8192], P(('dp', 'ctx'))
- grad_query: bfloat16 [8192, 8192], P(('dp', 'ctx'))
- grad_key: bfloat16 [8192, 1024], P(('dp', 'ctx'))
- grad_value: bfloat16 [8192, 1024], P(('dp', 'ctx'))
Inputs may be any that keep to these rules, and one draw needn't show every extreme that they name: `dest_rows`: A permutation of the learner rows; the 256 engine rows of each device hold exactly 8 rows for each device's 256 learner rows. `key_blocks`: each packed sequence is a run of token trees: a prompt of one or two blocks followed by two to four responses of one or two blocks each, the last tree possibly cut; the first tree has a prompt of two blocks and a first response of two blocks. For query block b the used entries, in increasing order, are the prompt blocks of b's tree and the blocks of b's own branch up to b itself; unused entries equal b. `key_count`: each packed sequence has a block that attends to 4 blocks. `key_rows`: keys of all heads.
All inputs are finite; a program needn't handle non-finite values.
Results may differ from a plain program's by a relative error of at most 0.02.
Values may be sent and summed in bfloat16 or wider, within the bound.
A program may use at most 192 MiB of HBM per device.

v0:
```python
import functools
import math

import jax
import jax.numpy as jnp
from jax import lax
from jax.experimental import pallas as pl
from jax.experimental.pallas import tpu as pltpu
from jax.sharding import PartitionSpec as P

HD = 128
BLK = 128
F32 = jnp.float32
BF16 = jnp.bfloat16
VMEM_LIMIT = 60 * 1024 * 1024


def chunk_sizes(heads):
    sizes, left = [], heads
    while left:
        sizes.append(min(len(sizes) + 1, left))
        left -= sizes[-1]
    return sizes[::-1]


def dot(a, b, ca, cb):
    return lax.dot_general(a, b, (((ca,), (cb,)), ((), ())), preferred_element_type=F32)


def send_order(dest_col, dest_row):
    rows = dest_col.shape[0]
    rank = jnp.sum((dest_col < dest_row).astype(jnp.int32), axis=0, keepdims=True)
    place = lax.broadcasted_iota(jnp.int32, (rows, rows), 0)
    return (place == rank).astype(F32).astype(BF16)


def prep_first_kernel(size, col_ref, row_ref, query_ref, grad_ref, key_ref, value_ref, out_ref):
    rows, width = key_ref.shape
    head_width = query_ref.shape[1] // size
    dest = col_ref[...]
    perm = send_order(dest, row_ref[...])

    def put(at, values):
        out_ref[:, at : at + values.shape[1]] = dot(perm, values, 1, 0).astype(BF16)
        return at + values.shape[1]

    at = 0
    for j in range(size):
        at = put(at, query_ref[:, j * head_width : (j + 1) * head_width])
        at = put(at, grad_ref[:, j * head_width : (j + 1) * head_width])
    at = put(at, key_ref[...])
    at = put(at, value_ref[...])
    slot = jnp.broadcast_to(lax.rem(dest, rows), (rows, HD))
    lane = lax.broadcasted_iota(jnp.int32, (rows, HD), 1)
    put(at, jnp.where(lane == 0, slot & 127, slot >> 7).astype(F32).astype(BF16))


def prep_qg_kernel(col_ref, row_ref, query_ref, grad_ref, out_ref):
    width = query_ref.shape[1]
    perm = send_order(col_ref[...], row_ref[...])
    out_ref[:, 0:width] = dot(perm, query_ref[...], 1, 0).astype(BF16)
    out_ref[:, width:] = dot(perm, grad_ref[...], 1, 0).astype(BF16)


def place_kernel(recv_ref, out_ref, perm_ref):
    rows, width = out_ref.shape
    end = recv_ref.shape[1] - HD
    slot = recv_ref[:, end : end + 1].astype(F32) + 128.0 * recv_ref[
        :, end + 1 : end + 2
    ].astype(F32)
    target = lax.broadcasted_iota(jnp.int32, (rows, rows), 1).astype(F32)
    perm = jnp.transpose((target == slot).astype(F32)).astype(BF16)
    perm_ref[...] = perm
    out_ref[...] = dot(perm, recv_ref[:, end - width : end], 1, 0).astype(BF16)


def finish_kernel(sizes, *refs):
    dk_ref, dv_ref = refs[-2:]
    rows = dk_ref.shape[0]
    head = 0
    for size, ref in zip(sizes, refs):
        total = ref[0:rows, :].astype(F32)
        for part in range(1, ref.shape[0] // rows):
            total = total + ref[part * rows : (part + 1) * rows, :].astype(F32)
        total = total.astype(BF16)
        for j in range(size):
            cols = slice(head * HD, (head + 1) * HD)
            dk_ref[:, cols] = total[:, 2 * j * HD : (2 * j + 1) * HD]
            dv_ref[:, cols] = total[:, (2 * j + 1) * HD : (2 * j + 2) * HD]
            head += 1


def attend_kernel(
    groups, slots, blocks_ref, count_ref, base_ref, perm_ref, qg_ref, key_ref, value_ref, *rest
):
    out_ref, dq_ref, dkv_ref, q_scr, g_scr, dk_scr, dv_scr = rest[-7:]
    rows = perm_ref.shape[0]
    width = groups * HD
    span = slots * BLK
    perm = perm_ref[...]
    q_scr[...] = dot(perm, qg_ref[:, 0:width], 1, 0).astype(BF16)
    g_scr[...] = dot(perm, qg_ref[:, width:], 1, 0).astype(BF16)
    dk_scr[...] = jnp.zeros_like(dk_scr)
    dv_scr[...] = jnp.zeros_like(dv_scr)
    scaling = 1.0 / math.sqrt(HD)
    scale2 = scaling * math.log2(math.e)
    pair = 2
    diff = lax.broadcasted_iota(jnp.int32, (BLK, BLK), 1) - lax.broadcasted_iota(
        jnp.int32, (BLK, BLK), 0
    )
    for b in range(rows // BLK):
        own = base_ref[0] + b
        count = count_ref[b]
        bias, starts = [], []
        for s in range(slots):
            blk = blocks_ref[b * slots + s]
            level = jnp.where(s < count, jnp.where(blk == own, 0, -BLK), BLK)
            bias.append(jnp.where(diff >= level, 0.0, -jnp.inf).astype(F32))
            starts.append(pl.multiple_of(blk * BLK, BLK))
        bias = jnp.concatenate(bias, axis=0)
        bias = jnp.concatenate([bias] * pair, axis=1)
        key_sel = jnp.concatenate([key_ref[pl.ds(at, BLK), :] for at in starts], axis=0)
        value_sel = jnp.concatenate([value_ref[pl.ds(at, BLK), :] for at in starts], axis=0)
        key_t = jnp.transpose(key_sel.astype(F32)).astype(BF16)
        value_t = jnp.transpose(value_sel.astype(F32)).astype(BF16)
        r0 = b * BLK
        dk = jnp.zeros((span, HD), F32)
        dv = jnp.zeros((span, HD), F32)
        for h in range(0, groups, pair):
            cols = [slice((h + i) * HD, (h + i + 1) * HD) for i in range(pair)]
            q2 = jnp.concatenate([q_scr[r0 : r0 + BLK, c] for c in cols], axis=0)
            g2 = jnp.concatenate([g_scr[r0 : r0 + BLK, c] for c in cols], axis=0)
            s_t = dot(key_sel, q2, 1, 1) * scale2 + bias
            dp_t = dot(value_sel, g2, 1, 1)
            e_t = jnp.exp2(s_t - jnp.max(s_t, axis=0, keepdims=True))
            p_t = e_t * (1.0 / jnp.sum(e_t, axis=0, keepdims=True))
            pb_t = p_t.astype(BF16)
            o_t = dot(value_t, pb_t, 1, 0)
            o_low = o_t.astype(BF16).astype(F32)
            delta = jnp.sum(jnp.transpose(g2.astype(F32)) * o_low, axis=0, keepdims=True)
            ds_t = (p_t * (dp_t - delta)).astype(BF16)
            dq_t = dot(key_t, ds_t, 1, 0) * scaling
            o_n = jnp.transpose(o_low).astype(BF16)
            dq_n = jnp.transpose(dq_t).astype(BF16)
            for i, c in enumerate(cols):
                out_ref[r0 : r0 + BLK, c] = o_n[i * BLK : (i + 1) * BLK]
                dq_ref[r0 : r0 + BLK, c] = dq_n[i * BLK : (i + 1) * BLK]
            dk = dk + dot(ds_t, q2, 1, 0)
            dv = dv + dot(pb_t, g2, 1, 0)
        for s, at in enumerate(starts):
            dk_scr[pl.ds(at, BLK), :] += dk[s * BLK : (s + 1) * BLK]
            dv_scr[pl.ds(at, BLK), :] += dv[s * BLK : (s + 1) * BLK]
    dkv_ref[:, 0:HD] = (dk_scr[...] * scaling).astype(BF16)
    dkv_ref[:, HD:] = dv_scr[...].astype(BF16)


def body(query_rows, key_rows, value_rows, grad_out, dest_rows, key_blocks, key_count):
    peers = lax.axis_size("dp") * lax.axis_size("ctx")
    rows, q_width = query_rows.shape
    kv_width = key_rows.shape[1]
    kv_heads = kv_width // HD
    groups = q_width // kv_width
    head_width = groups * HD
    local_blocks, slots = key_blocks.shape[1:]
    seq = rows * lax.axis_size("ctx")
    dest_col = dest_rows.reshape(rows, 1)
    dest_row = dest_rows.reshape(1, rows)
    params = pltpu.CompilerParams(vmem_limit_bytes=VMEM_LIMIT)

    def exchange(x):
        y = lax.all_to_all(
            x.reshape(peers, rows // peers, x.shape[1]),
            ("dp", "ctx"),
            split_axis=0,
            concat_axis=0,
            tiled=True,
        )
        return y.reshape(rows, x.shape[1])

    sizes = chunk_sizes(kv_heads)
    head_cols = sizes[0] * head_width
    sent = pl.pallas_call(
        functools.partial(prep_first_kernel, sizes[0]),
        grid=(1,),
        in_specs=[
            pl.BlockSpec((rows, 1), lambda j: (0, 0)),
            pl.BlockSpec((1, rows), lambda j: (0, 0)),
            pl.BlockSpec((rows, head_cols), lambda j: (0, 0)),
            pl.BlockSpec((rows, head_cols), lambda j: (0, 0)),
            pl.BlockSpec((rows, kv_width), lambda j: (0, 0)),
            pl.BlockSpec((rows, kv_width), lambda j: (0, 0)),
        ],
        out_specs=pl.BlockSpec((rows, 2 * head_cols + 2 * kv_width + HD), lambda j: (0, 0)),
        out_shape=jax.ShapeDtypeStruct((rows, 2 * head_cols + 2 * kv_width + HD), BF16),
        compiler_params=params,
        name="prep_first",
    )(dest_col, dest_row, query_rows, grad_out, key_rows, value_rows)
    received = [exchange(sent)]
    first = sizes[0]
    for size in sizes[1:]:
        sent = pl.pallas_call(
            prep_qg_kernel,
            grid=(size,),
            in_specs=[
                pl.BlockSpec((rows, 1), lambda j: (0, 0)),
                pl.BlockSpec((1, rows), lambda j: (0, 0)),
                pl.BlockSpec((rows, head_width), lambda j, f=first: (0, f + j)),
                pl.BlockSpec((rows, head_width), lambda j, f=first: (0, f + j)),
            ],
            out_specs=pl.BlockSpec((rows, 2 * head_width), lambda j: (0, j)),
            out_shape=jax.ShapeDtypeStruct((rows, size * 2 * head_width), BF16),
            compiler_params=params,
            cost_estimate=pl.CostEstimate(
                flops=4 * rows * rows * size * head_width,
                bytes_accessed=8 * rows * size * head_width,
                transcendentals=0,
            ),
            name="prep_qg",
        )(dest_col, dest_row, query_rows, grad_out)
        received.append(exchange(sent))
        first += size

    placed, perm = pl.pallas_call(
        place_kernel,
        out_shape=(
            jax.ShapeDtypeStruct((rows, 2 * kv_width), BF16),
            jax.ShapeDtypeStruct((rows, rows), BF16),
        ),
        compiler_params=params,
        name="place_kv",
    )(received[0])
    kv_all = lax.all_gather(placed, "ctx", axis=0, tiled=True)

    block_list = key_blocks.reshape(local_blocks * slots)
    counts = key_count.reshape(local_blocks)
    base = (lax.axis_index("ctx") * local_blocks).astype(jnp.int32).reshape(1)
    out = dq = None
    sums = []
    first = 0
    for size, recv in zip(sizes, received):
        operands = [perm, recv, kv_all, kv_all]
        in_specs = [
            pl.BlockSpec((rows, rows), lambda j, *_: (0, 0)),
            pl.BlockSpec((rows, 2 * head_width), lambda j, *_: (0, j)),
            pl.BlockSpec((seq, HD), lambda j, *_, f=first: (0, f + j)),
            pl.BlockSpec((seq, HD), lambda j, *_, f=first: (0, kv_heads + f + j)),
        ]
        aliases = {}
        if out is not None:
            aliases = {7: 0, 8: 1}
            operands += [out, dq]
            in_specs += [pl.BlockSpec(memory_space=pl.ANY)] * 2
        out, dq, dkv = pl.pallas_call(
            functools.partial(attend_kernel, groups, slots),
            grid_spec=pltpu.PrefetchScalarGridSpec(
                num_scalar_prefetch=3,
                grid=(size,),
                in_specs=in_specs,
                out_specs=[
                    pl.BlockSpec((rows, head_width), lambda j, *_, f=first: (0, f + j)),
                    pl.BlockSpec((rows, head_width), lambda j, *_, f=first: (0, f + j)),
                    pl.BlockSpec((seq, 2 * HD), lambda j, *_: (0, j)),
                ],
                scratch_shapes=[
                    pltpu.VMEM((rows, head_width), BF16),
                    pltpu.VMEM((rows, head_width), BF16),
                    pltpu.VMEM((seq, HD), F32),
                    pltpu.VMEM((seq, HD), F32),
                ],
            ),
            out_shape=(
                jax.ShapeDtypeStruct((rows, q_width), BF16),
                jax.ShapeDtypeStruct((rows, q_width), BF16),
                jax.ShapeDtypeStruct((seq, size * 2 * HD), BF16),
            ),
            input_output_aliases=aliases,
            compiler_params=params,
            cost_estimate=pl.CostEstimate(
                flops=20 * rows * slots * BLK * size * head_width,
                bytes_accessed=8 * rows * size * head_width + 8 * seq * size * HD,
                transcendentals=rows * slots * BLK * size * groups,
            ),
            name="attend",
        )(block_list, counts, base, *operands)
        if first + size < kv_heads:
            sums.append(lax.psum_scatter(dkv, "ctx", scatter_dimension=0, tiled=True))
        else:
            sums.append(lax.all_to_all(dkv, "ctx", split_axis=0, concat_axis=0, tiled=True))
        first += size

    dk, dv = pl.pallas_call(
        functools.partial(finish_kernel, sizes),
        out_shape=(jax.ShapeDtypeStruct((rows, kv_width), BF16),) * 2,
        compiler_params=params,
        name="finish",
    )(*sums)
    return out, dq, dk, dv


def solution(mesh):
    split = P(("dp", "ctx"), None)
    return jax.shard_map(
        body,
        mesh=mesh,
        in_specs=(
            split,
            split,
            split,
            split,
            P(("dp", "ctx")),
            P("dp", "ctx", None),
            P("dp", "ctx"),
        ),
        out_specs=(split, split, split, split),
        check_vma=False,
    )
```

profile of v0, /device:TPU:0, one launch (start us, length us, event | category | flops | bytes accessed | tf_op | source)
XLA Modules:
  0.0 339.9 jit_solution(6036916318261056090)
XLA Ops:
  7.2 1.5 copy.17.col_ref
  8.6 4.7 %prep_first.1 = bf16[256,6272]{1,0:T(8,128)(2,1)} custom-call(s32[256,1]{1,0:T(8,128)} %copy.17.col_ref, s32[1,256]{1,0:T(1,128)} %bitcast.25, bf16[256,8192]{1,0:T(8,128)(2,1)} %query_ref.7, bf16[256,8192]{1,0:T(8,128)(2,1)} %grad_ref.7, bf16[256,1024]{1,0:T(8,128)(2,1)} %key_ref.1, bf16[256,1024]{1,0:T(8,128)(2,1)} %value_ref.1), custom_call_target="tpu_custom_call" | custom-call | tf_op jit(solution)/shard_map/prep_first/pallas_call | solution.py:182
  13.3 7.3 %all-to-all-start = ((bf16[32,8,6272]{2,1,0:T(8,128)(2,1)}), bf16[32,8,6272]{2,1,0:T(8,128)(2,1)S(1)}, u32[]{:S(2)}, u32[]{:S(2)}) async-start(bf16[32,8,6272]{2,1,0:T(8,128)(2,1)} %bitcast.16), calls=%async_computation | async-start | bytes 6422528 | tf_op jit(solution)/shard_map/all_to_all | solution.py:171
  20.6 5.2 %prep_qg.5 = bf16[256,6144]{1,0:T(8,128)(2,1)} custom-call(s32[256,1]{1,0:T(8,128)} %copy.17.col_ref, s32[1,256]{1,0:T(1,128)} %bitcast.26, bf16[256,8192]{1,0:T(8,128)(2,1)} %query_ref.7, bf16[256,8192]{1,0:T(8,128)(2,1)} %grad_ref.7), custom_call_target="tpu_custom_call" | custom-call | flops 805306368 | bytes 6291456 | tf_op jit(solution)/shard_map/prep_qg/pallas_call | solution.py:201
  25.9 67.6 %all-to-all-done = bf16[32,8,6272]{2,1,0:T(8,128)(2,1)S(1)} async-done(((bf16[32,8,6272]{2,1,0:T(8,128)(2,1)}), bf16[32,8,6272]{2,1,0:T(8,128)(2,1)S(1)}, u32[]{:S(2)}, u32[]{:S(2)}) %all-to-all-start) | async-done | bytes 3211296 | tf_op jit(solution)/shard_map/all_to_all | solution.py:171
  93.5 0.0 copy-start
  93.5 4.1 %all-to-all-start.3 = ((bf16[32,8,6144]{2,1,0:T(8,128)(2,1)}), bf16[32,8,6144]{2,1,0:T(8,128)(2,1)}, u32[]{:S(2)}, u32[]{:S(2)}) async-start(bf16[32,8,6144]{2,1,0:T(8,128)(2,1)} %bitcast.17), calls=%async_computation.3 | async-start | bytes 6291456 | tf_op jit(solution)/shard_map/all_to_all | solution.py:171
  97.5 0.0 all-gather.2.cloned.1.call-start
  97.6 0.0 copy-done
  97.6 3.5 %place_kv.1 = (bf16[256,2048]{1,0:T(8,128)(2,1)}, bf16[256,256]{1,0:T(8,128)(2,1)}) custom-call(bf16[256,6272]{1,0:T(8,128)(2,1)} %bitcast.14), custom_call_target="tpu_custom_call" | custom-call | tf_op jit(solution)/shard_map/place_kv/pallas_call | solution.py:223
  101.1 0.0 all-gather.2.cloned.1.call-update
  101.1 3.4 prep_qg.4
  104.5 0.0 copy-start.2
  104.5 64.6 %all-to-all-done.3 = bf16[32,8,6144]{2,1,0:T(8,128)(2,1)} async-done(((bf16[32,8,6144]{2,1,0:T(8,128)(2,1)}), bf16[32,8,6144]{2,1,0:T(8,128)(2,1)}, u32[]{:S(2)}, u32[]{:S(2)}) %all-to-all-start.3) | async-done | bytes 3145760 | tf_op jit(solution)/shard_map/all_to_all | solution.py:171
  169.1 3.8 %all-to-all-start.2 = ((bf16[32,8,4096]{2,1,0:T(8,128)(2,1)}), bf16[32,8,4096]{2,1,0:T(8,128)(2,1)S(1)}, u32[]{:S(2)}, u32[]{:S(2)}) async-start(bf16[32,8,4096]{2,1,0:T(8,128)(2,1)} %bitcast.18), calls=%async_computation.2 | async-start | bytes 4194304 | tf_op jit(solution)/shard_map/all_to_all | solution.py:171
  173.0 0.0 reduce-scatter.8.cloned.1.call-start
  173.0 0.0 copy-done.2
  173.0 0.6 reshape.49.blocks_ref
  173.6 0.0 all-gather.2.cloned.1.call-done.key_ref.value_ref
  173.7 16.8 %attend.4 = (bf16[256,8192]{1,0:T(8,128)(2,1)}, bf16[256,8192]{1,0:T(8,128)(2,1)}, bf16[1024,512]{1,0:T(8,128)(2,1)}) custom-call(s32[8]{0:T(128)} %reshape.49.blocks_ref, s32[2]{0:T(128)} %bitcast.29, s32[1]{0:T(128)} %bitcast.1.base_ref, bf16[256,256]{1,0:T(8,128)(2,1)} %get-tuple-element.20.perm_ref, bf16[256,6272]{1,0:T(8,128)(2,1)} %bitcast.15, ...), custom_call_target="tpu_custom_call" | custom-call | flops 5368709120 | bytes 6291456 | tf_op jit(solution)/shard_map/attend/pallas_call | solution.py:253
  190.5 24.0 %attend.5 = (bf16[256,8192]{1,0:T(8,128)(2,1)}, bf16[256,8192]{1,0:T(8,128)(2,1)}, bf16[1024,768]{1,0:T(8,128)(2,1)}) custom-call(s32[8]{0:T(128)} %reshape.49.blocks_ref, s32[2]{0:T(128)} %bitcast.30, s32[1]{0:T(128)} %bitcast.1.base_ref, bf16[256,256]{1,0:T(8,128)(2,1)} %get-tuple-element.20.perm_ref, ...), custom_call_target="tpu_custom_call", output_to_operand_aliasing={{0}: (7, {}), {1}: (8, {})} | custom-call | flops 8053063680 | bytes 9437184 | tf_op jit(solution)/shard_map/attend/pallas_call | solution.py:253
  214.5 7.4 %all-to-all-done.2 = bf16[32,8,4096]{2,1,0:T(8,128)(2,1)S(1)} async-done(((bf16[32,8,4096]{2,1,0:T(8,128)(2,1)}), bf16[32,8,4096]{2,1,0:T(8,128)(2,1)S(1)}, u32[]{:S(2)}, u32[]{:S(2)}) %all-to-all-start.2) | async-done | bytes 2097184 | tf_op jit(solution)/shard_map/all_to_all | solution.py:171
  221.9 0.0 copy-start.1
  221.9 1.4 copy-done.1
  223.2 17.1 %attend.6 = (bf16[256,8192]{1,0:T(8,128)(2,1)}, bf16[256,8192]{1,0:T(8,128)(2,1)}, bf16[1024,512]{1,0:T(8,128)(2,1)}) custom-call(s32[8]{0:T(128)} %reshape.49.blocks_ref, s32[2]{0:T(128)} %bitcast.31, s32[1]{0:T(128)} %bitcast.1.base_ref, bf16[256,256]{1,0:T(8,128)(2,1)} %get-tuple-element.20.perm_ref, ...), custom_call_target="tpu_custom_call", output_to_operand_aliasing={{0}: (7, {}), {1}: (8, {})} | custom-call | flops 5368709120 | bytes 6291456 | tf_op jit(solution)/shard_map/attend/pallas_call | solution.py:253
  240.4 0.0 reduce-scatter.8.cloned.1.call-update
  240.4 0.0 reduce-scatter.4.cloned.1.call-start
  240.5 0.7 reduce-scatter.4.cloned.1.call-update
  241.2 0.0 reduce-scatter.6.cloned.1.call-start
  241.2 0.5 reduce-scatter.6.cloned.1.call-update
  241.7 2.8 prep_qg.3
  244.6 30.4 %all_to_all.31 = bf16[32,8,2048]{2,1,0:T(8,128)(2,1)} all-to-all(bf16[32,8,2048]{2,1,0:T(8,128)(2,1)} %bitcast.19), channel_id=1, replica_groups=mesh['dp'=8,'ctx'=4] {'dp','ctx'}, dimensions={0} | all-to-all | bytes 2097152 | tf_op jit(solution)/shard_map/all_to_all | solution.py:171
  274.9 9.9 %attend.7 = (bf16[256,8192]{1,0:T(8,128)(2,1)}, bf16[256,8192]{1,0:T(8,128)(2,1)}, bf16[1024,256]{1,0:T(8,128)(2,1)}) custom-call(s32[8]{0:T(128)} %reshape.49.blocks_ref, s32[2]{0:T(128)} %bitcast.32, s32[1]{0:T(128)} %bitcast.1.base_ref, bf16[256,256]{1,0:T(8,128)(2,1)} %get-tuple-element.20.perm_ref, ...), custom_call_target="tpu_custom_call", output_to_operand_aliasing={{0}: (7, {}), {1}: (8, {})} | custom-call | flops 2684354560 | bytes 3145728 | tf_op jit(solution)/shard_map/attend/pallas_call | solution.py:253
  284.8 15.3 %all_to_all.32 = bf16[4,256,256]{2,1,0:T(8,128)(2,1)} all-to-all(bf16[4,256,256]{2,1,0:T(8,128)(2,1)} %bitcast.23), channel_id=1, replica_groups=mesh['dp'=8,'ctx'=4] {'ctx'}, dimensions={0} | all-to-all | bytes 1048576 | tf_op jit(solution)/shard_map/all_to_all | solution.py:288
  300.2 0.0 reduce-scatter.8.cloned.1.call-done.refs_2_
  300.2 0.0 reduce-scatter.4.cloned.1.call-done.refs_0_
  300.2 30.6 %reduce-scatter.6.cloned.1.call-done.refs_1_ = bf16[256,768]{1,0:T(8,128)(2,1)} async-done(((bf16[1024,768]{1,0:T(8,128)(2,1)}), bf16[256,768]{1,0:T(8,128)(2,1)}) %reduce-scatter.6.cloned.1.call-update) | async-done | bytes 393232 | tf_op jit(solution)/shard_map/reduce_scatter | solution.py:286
  330.8 2.6 finish.1
Async XLA Ops:
  13.3 80.2 %all-to-all-start = ((bf16[32,8,6272]{2,1,0:T(8,128)(2,1)}), bf16[32,8,6272]{2,1,0:T(8,128)(2,1)S(1)}, u32[]{:S(2)}, u32[]{:S(2)}) async-start(bf16[32,8,6272]{2,1,0:T(8,128)(2,1)} %bitcast.16), calls=%async_computation | async-start | bytes 6422528 | tf_op jit(solution)/shard_map/all_to_all | solution.py:171
  93.5 4.1 %copy-start = (bf16[32,8,6272]{2,1,0:T(8,128)(2,1)}, bf16[32,8,6272]{2,1,0:T(8,128)(2,1)S(1)}, u32[]{:S(2)}) copy-start(bf16[32,8,6272]{2,1,0:T(8,128)(2,1)S(1)} %all-to-all-done) | copy-start | bytes 9633796
  93.5 75.7 %all-to-all-start.3 = ((bf16[32,8,6144]{2,1,0:T(8,128)(2,1)}), bf16[32,8,6144]{2,1,0:T(8,128)(2,1)}, u32[]{:S(2)}, u32[]{:S(2)}) async-start(bf16[32,8,6144]{2,1,0:T(8,128)(2,1)} %bitcast.17), calls=%async_computation.3 | async-start | bytes 6291456 | tf_op jit(solution)/shard_map/all_to_all | solution.py:171
  97.5 76.1 %all-gather.2.cloned.1.call-start = ((), (), s32[]{:S(2)}) async-start(), calls=%async_computation.8 | async-start | bytes 5242880 | tf_op jit(solution)/shard_map/all_gather | solution.py:232
  104.5 68.5 %copy-start.2 = (s32[1,2,4]{2,1,0:T(2,128)S(1)}, s32[1,2,4]{2,1,0:T(2,128)}, u32[]{:S(2)}) copy-start(s32[1,2,4]{2,1,0:T(2,128)} %param.12) | copy-start | bytes 100
  169.1 52.7 %all-to-all-start.2 = ((bf16[32,8,4096]{2,1,0:T(8,128)(2,1)}), bf16[32,8,4096]{2,1,0:T(8,128)(2,1)S(1)}, u32[]{:S(2)}, u32[]{:S(2)}) async-start(bf16[32,8,4096]{2,1,0:T(8,128)(2,1)} %bitcast.18), calls=%async_computation.2 | async-start | bytes 4194304 | tf_op jit(solution)/shard_map/all_to_all | solution.py:171
  173.0 127.2 %reduce-scatter.8.cloned.1.call-start = ((), (), s32[]{:S(2)}) async-start(), calls=%async_computation.11 | async-start | bytes 1310720 | tf_op jit(solution)/shard_map/reduce_scatter | solution.py:286
  221.9 1.4 copy-start.1
  240.4 59.8 %reduce-scatter.4.cloned.1.call-start = ((), (), s32[]{:S(2)}) async-start(), calls=%async_computation.9 | async-start | bytes 1310720 | tf_op jit(solution)/shard_map/reduce_scatter | solution.py:286
  241.2 89.6 %reduce-scatter.6.cloned.1.call-start = ((), (), s32[]{:S(2)}) async-start(), calls=%async_computation.10 | async-start | bytes 1966080 | tf_op jit(solution)/shard_map/reduce_scatter | solution.py:286
Sparse Core Ops, SparseCore 0:
  101.3 52.5 all-gather.1
  240.5 28.0 reduce-scatter.7
  271.3 26.4 reduce-scatter.3
  300.2 30.5 reduce-scatter.5
where the time goes:
time: 341 us; the launch traced here: 340 us
  waiting for transfers between devices  171 us (50%)
  Pallas kernels  90.1 us (26%)
  blocking collectives  45.7 us (13%)
  starting transfers between devices  15.3 us (4%)
  between operations  13.8 us (4%)
  local copies, waits for them, and re-layouts  3.45 us (1%)
    all_to_all x3, waiting for transfers between devices, exchange(): lax.all_to_all(x.reshape(peers, rows // peers, x.shape[1]), ('dp', 'ctx')...  140 us
    pallas_call x4, Pallas kernels, body(): pl.pallas_call(functools.partial(attend_kernel, groups, slots), grid_spec...  67.9 us
    reduce_scatter x3, waiting for transfers between devices, body(): sums.append(lax.psum_scatter(dkv, 'ctx', scatter_dimension=0, tiled=True))  30.6 us
    all_to_all x1, blocking collectives, exchange(): lax.all_to_all(x.reshape(peers, rows // peers, x.shape[1]), ('dp', 'ctx')...  30.4 us
    all_to_all x1, blocking collectives, body(): lax.all_to_all(dkv, 'ctx', split_axis=0, concat_axis=0, tiled=True)  15.3 us
    all_to_all x3, starting transfers between devices, exchange(): lax.all_to_all(x.reshape(peers, rows // peers, x.shape[1]), ('dp', 'ctx')...  15.2 us
    pallas_call x3, Pallas kernels, body(): pl.pallas_call(prep_qg_kernel, grid=(size,), in_specs=[pl.BlockSpec((rows...  11.5 us
  transfers between devices with their start and end apart: 7, of which 4 were waited for; matrix products, arithmetic and copies ran while one was open for 0% of the time, Pallas kernels for 19%

commit v1 on v0

--- a/solution.py
+++ b/solution.py
@@ -15,12 +15,13 @@
 VMEM_LIMIT = 60 * 1024 * 1024
 
 
+TAIL = 2
+
+
 def chunk_sizes(heads):
-    sizes, left = [], heads
-    while left:
-        sizes.append(min(len(sizes) + 1, left))
-        left -= sizes[-1]
-    return sizes[::-1]
+    if heads < 4:
+        return [1] * heads
+    return [heads // 4, heads - heads // 4 - TAIL, 1, 1]
 
 
 def dot(a, b, ca, cb):
@@ -196,16 +197,27 @@
         name="prep_first",
     )(dest_col, dest_row, query_rows, grad_out, key_rows, value_rows)
     received = [exchange(sent)]
-    first = sizes[0]
-    for size in sizes[1:]:
-        sent = pl.pallas_call(
+    placed, perm = pl.pallas_call(
+        place_kernel,
+        out_shape=(
+            jax.ShapeDtypeStruct((rows, 2 * kv_width), BF16),
+            jax.ShapeDtypeStruct((rows, rows), BF16),
+        ),
+        compiler_params=params,
+        name="place_kv",
+    )(received[0])
+    kv_all = lax.all_gather(placed, "ctx", axis=0, tiled=True)
+
+    def send(c):
+        first, size = sum(sizes[:c]), sizes[c]
+        return pl.pallas_call(
             prep_qg_kernel,
             grid=(size,),
             in_specs=[
                 pl.BlockSpec((rows, 1), lambda j: (0, 0)),
                 pl.BlockSpec((1, rows), lambda j: (0, 0)),
-                pl.BlockSpec((rows, head_width), lambda j, f=first: (0, f + j)),
-                pl.BlockSpec((rows, head_width), lambda j, f=first: (0, f + j)),
+                pl.BlockSpec((rows, head_width), lambda j: (0, first + j)),
+                pl.BlockSpec((rows, head_width), lambda j: (0, first + j)),
             ],
             out_specs=pl.BlockSpec((rows, 2 * head_width), lambda j: (0, j)),
             out_shape=jax.ShapeDtypeStruct((rows, size * 2 * head_width), BF16),
@@ -217,49 +229,36 @@
             ),
             name="prep_qg",
         )(dest_col, dest_row, query_rows, grad_out)
-        received.append(exchange(sent))
-        first += size
-
-    placed, perm = pl.pallas_call(
-        place_kernel,
-        out_shape=(
-            jax.ShapeDtypeStruct((rows, 2 * kv_width), BF16),
-            jax.ShapeDtypeStruct((rows, rows), BF16),
-        ),
-        compiler_params=params,
-        name="place_kv",
-    )(received[0])
-    kv_all = lax.all_gather(placed, "ctx", axis=0, tiled=True)
 
     block_list = key_blocks.reshape(local_blocks * slots)
     counts = key_count.reshape(local_blocks)
     base = (lax.axis_index("ctx") * local_blocks).astype(jnp.int32).reshape(1)
-    out = dq = None
-    sums = []
-    first = 0
-    for size, recv in zip(sizes, received):
+
+    def attend(c, recv, out, dq, dkv, dkv_heads, dkv_first):
+        first, size = sum(sizes[:c]), sizes[c]
         operands = [perm, recv, kv_all, kv_all]
         in_specs = [
             pl.BlockSpec((rows, rows), lambda j, *_: (0, 0)),
             pl.BlockSpec((rows, 2 * head_width), lambda j, *_: (0, j)),
-            pl.BlockSpec((seq, HD), lambda j, *_, f=first: (0, f + j)),
-            pl.BlockSpec((seq, HD), lambda j, *_, f=first: (0, kv_heads + f + j)),
+            pl.BlockSpec((seq, HD), lambda j, *_: (0, first + j)),
+            pl.BlockSpec((seq, HD), lambda j, *_: (0, kv_heads + first + j)),
         ]
         aliases = {}
-        if out is not None:
-            aliases = {7: 0, 8: 1}
-            operands += [out, dq]
-            in_specs += [pl.BlockSpec(memory_space=pl.ANY)] * 2
-        out, dq, dkv = pl.pallas_call(
+        for place, array in enumerate((out, dq, dkv)):
+            if array is not None:
+                aliases[3 + len(operands)] = place
+                operands.append(array)
+                in_specs.append(pl.BlockSpec(memory_space=pl.ANY))
+        return pl.pallas_call(
             functools.partial(attend_kernel, groups, slots),
             grid_spec=pltpu.PrefetchScalarGridSpec(
                 num_scalar_prefetch=3,
                 grid=(size,),
                 in_specs=in_specs,
                 out_specs=[
-                    pl.BlockSpec((rows, head_width), lambda j, *_, f=first: (0, f + j)),
-                    pl.BlockSpec((rows, head_width), lambda j, *_, f=first: (0, f + j)),
-                    pl.BlockSpec((seq, 2 * HD), lambda j, *_: (0, j)),
+                    pl.BlockSpec((rows, head_width), lambda j, *_: (0, first + j)),
+                    pl.BlockSpec((rows, head_width), lambda j, *_: (0, first + j)),
+                    pl.BlockSpec((seq, 2 * HD), lambda j, *_: (0, dkv_first + j)),
                 ],
                 scratch_shapes=[
                     pltpu.VMEM((rows, head_width), BF16),
@@ -271,7 +270,7 @@
             out_shape=(
                 jax.ShapeDtypeStruct((rows, q_width), BF16),
                 jax.ShapeDtypeStruct((rows, q_width), BF16),
-                jax.ShapeDtypeStruct((seq, size * 2 * HD), BF16),
+                jax.ShapeDtypeStruct((seq, dkv_heads * 2 * HD), BF16),
             ),
             input_output_aliases=aliases,
             compiler_params=params,
@@ -282,14 +281,36 @@
             ),
             name="attend",
         )(block_list, counts, base, *operands)
-        if first + size < kv_heads:
-            sums.append(lax.psum_scatter(dkv, "ctx", scatter_dimension=0, tiled=True))
+
+    chunks = len(sizes)
+    tail_from = max(chunks - TAIL, 0)
+    tail_sizes = sizes[tail_from:]
+    sums = [None] * tail_from
+    out = dq = tail = None
+    for c in range(chunks):
+        if c + 1 < chunks:
+            sent = send(c + 1)
+            if c >= 1:
+                held = sums[: min(c - 1, tail_from)]
+                sent, dkv, held = lax.optimization_barrier((sent, dkv, held))
+                sums[: len(held)] = held
+                if c - 1 < tail_from:
+                    sums[c - 1] = lax.psum_scatter(dkv, "ctx", scatter_dimension=0, tiled=True)
+                else:
+                    tail = dkv
+            received.append(exchange(sent))
+        elif 0 <= c - 1 < tail_from:
+            sums[c - 1] = lax.psum_scatter(dkv, "ctx", scatter_dimension=0, tiled=True)
+        if c < tail_from:
+            out, dq, dkv = attend(c, received[c], out, dq, None, sizes[c], 0)
         else:
-            sums.append(lax.all_to_all(dkv, "ctx", split_axis=0, concat_axis=0, tiled=True))
-        first += size
+            done = sum(sizes[tail_from:c])
+            out, dq, dkv = attend(c, received[c], out, dq, tail, sum(tail_sizes), done)
+            tail = dkv
+    sums.append(lax.all_to_all(tail, "ctx", split_axis=0, concat_axis=0, tiled=True))
 
     dk, dv = pl.pallas_call(
-        functools.partial(finish_kernel, sizes),
+        functools.partial(finish_kernel, sizes[:tail_from] + [sum(tail_sizes)]),
         out_shape=(jax.ShapeDtypeStruct((rows, kv_width), BF16),) * 2,
         compiler_params=params,
         name="finish",

time: 341 us -> 300 us (0.88)
  blocking collectives: 45.7 us -> 18.8 us
  waiting for transfers between devices: 171 us -> 151 us
  starting transfers between devices: 15.3 us -> 21.5 us
    all_gather x1, waiting for transfers between devices: 0.01 us -> 59.1 us  [body(): kv_all = lax.all_gather(placed, 'ctx', axis=0, tiled=True)]
    all_to_all x3 -> x4, waiting for transfers between devices: 140 us -> 91.4 us  [exchange(): lax.all_to_all(x.reshape(peers, rows // peers, x.shape[1]), ('dp', 'ctx')...]
    reduce_scatter x3 -> x2, waiting for transfers between devices: 30.6 us -> 0.01 us  [body(): sums[c - 1] = lax.psum_scatter(dkv, 'ctx', scatter_dimension=0, tiled=True)]
    all_to_all x2 -> x1, blocking collectives: 45.7 us -> 18.8 us  [body(): lax.all_to_all(tail, 'ctx', split_axis=0, concat_axis=0, tiled=True)]
    all_to_all x3 -> x4, starting transfers between devices: 15.2 us -> 21.2 us  [exchange(): lax.all_to_all(x.reshape(peers, rows // peers, x.shape[1]), ('dp', 'ctx')...]
  transfers between devices with their start and end apart: 7 -> 7, of which waited for: 4 -> 4; matrix products, arithmetic and copies ran while one was open for 0% -> 0% of each run, Pallas kernels for 19% -> 28%
where the time goes in v1:
time: 300 us; the launch traced here: 299 us
  waiting for transfers between devices  151 us (50%)
  Pallas kernels  89.8 us (30%)
  starting transfers between devices  21.5 us (7%)
  blocking collectives  18.8 us (6%)
  between operations  13.8 us (5%)
  local copies, waits for them, and re-layouts  4.77 us (2%)
    all_to_all x4, waiting for transfers between devices, exchange(): lax.all_to_all(x.reshape(peers, rows // peers, x.shape[1]), ('dp', 'ctx')...  91.4 us
    pallas_call x4, Pallas kernels, attend(): pl.pallas_call(functools.partial(attend_kernel, groups, slots), grid_spec...  67.5 us
    all_gather x1, waiting for transfers between devices, body(): kv_all = lax.all_gather(placed, 'ctx', axis=0, tiled=True)  59.1 us
    all_to_all x4, starting transfers between devices, exchange(): lax.all_to_all(x.reshape(peers, rows // peers, x.shape[1]), ('dp', 'ctx')...  21.2 us
    all_to_all x1, blocking collectives, body(): lax.all_to_all(tail, 'ctx', split_axis=0, concat_axis=0, tiled=True)  18.8 us
    pallas_call x3, Pallas kernels, send(): pl.pallas_call(prep_qg_kernel, grid=(size,), in_specs=[pl.BlockSpec((rows...  11.4 us
  transfers between devices with their start and end apart: 7, of which 4 were waited for; matrix products, arithmetic and copies ran while one was open for 0% of the time, Pallas kernels for 28%

profile of v1, /device:TPU:0, one launch (start us, length us, event | category | flops | bytes accessed | tf_op | source)
XLA Modules:
  0.0 299.2 jit_solution(18012151711961392501)
XLA Ops:
  7.2 1.5 copy.18.col_ref
  8.6 4.7 %prep_first.1 = bf16[256,6272]{1,0:T(8,128)(2,1)} custom-call(s32[256,1]{1,0:T(8,128)} %copy.18.col_ref, s32[1,256]{1,0:T(1,128)} %bitcast.23, bf16[256,8192]{1,0:T(8,128)(2,1)} %query_ref.7, bf16[256,8192]{1,0:T(8,128)(2,1)} %grad_ref.7, bf16[256,1024]{1,0:T(8,128)(2,1)} %key_ref.1, bf16[256,1024]{1,0:T(8,128)(2,1)} %value_ref.1), custom_call_target="tpu_custom_call" | custom-call | tf_op jit(solution)/shard_map/prep_first/pallas_call | solution.py:183
  13.3 7.3 %all-to-all-start = ((bf16[32,8,6272]{2,1,0:T(8,128)(2,1)}), bf16[32,8,6272]{2,1,0:T(8,128)(2,1)S(1)}, u32[]{:S(2)}, u32[]{:S(2)}) async-start(bf16[32,8,6272]{2,1,0:T(8,128)(2,1)} %bitcast.17), calls=%async_computation | async-start | bytes 6422528 | tf_op jit(solution)/shard_map/all_to_all | solution.py:172
  20.6 5.8 %prep_qg.4 = bf16[256,8192]{1,0:T(8,128)(2,1)} custom-call(s32[256,1]{1,0:T(8,128)} %copy.18.col_ref, s32[1,256]{1,0:T(1,128)} %bitcast.24, bf16[256,8192]{1,0:T(8,128)(2,1)} %query_ref.7, bf16[256,8192]{1,0:T(8,128)(2,1)} %grad_ref.7), custom_call_target="tpu_custom_call" | custom-call | flops 1073741824 | bytes 8388608 | tf_op jit(solution)/shard_map/prep_qg/pallas_call | solution.py:213
  26.4 67.0 %all-to-all-done = bf16[32,8,6272]{2,1,0:T(8,128)(2,1)S(1)} async-done(((bf16[32,8,6272]{2,1,0:T(8,128)(2,1)}), bf16[32,8,6272]{2,1,0:T(8,128)(2,1)S(1)}, u32[]{:S(2)}, u32[]{:S(2)}) %all-to-all-start) | async-done | bytes 3211296 | tf_op jit(solution)/shard_map/all_to_all | solution.py:172
  93.5 0.0 copy-start
  93.5 1.7 copy-done
  95.1 4.1 %all-to-all-start.1 = ((bf16[32,8,8192]{2,1,0:T(8,128)(2,1)}), bf16[32,8,8192]{2,1,0:T(8,128)(2,1)}, u32[]{:S(2)}, u32[]{:S(2)}) async-start(bf16[32,8,8192]{2,1,0:T(8,128)(2,1)} %bitcast.14), calls=%async_computation.1 | async-start | bytes 8388608 | tf_op jit(solution)/shard_map/all_to_all | solution.py:172
  99.2 0.0 copy-start.3
  99.2 0.0 all-gather.2.cloned.1.call-start
  99.3 3.5 %place_kv.1 = (bf16[256,2048]{1,0:T(8,128)(2,1)}, bf16[256,256]{1,0:T(8,128)(2,1)}) custom-call(bf16[256,6272]{1,0:T(8,128)(2,1)} %bitcast.15), custom_call_target="tpu_custom_call" | custom-call | tf_op jit(solution)/shard_map/place_kv/pallas_call | solution.py:200
  102.8 0.0 all-gather.2.cloned.1.call-update
  102.8 0.0 reduce-scatter.3.cloned.1.call-start
  102.9 0.0 copy-done.3
  102.9 0.6 reshape.49.blocks_ref
  103.5 2.8 prep_qg.5
  106.3 59.1 %all-gather.2.cloned.1.call-done.key_ref.value_ref = bf16[1024,2048]{1,0:T(8,128)(2,1)} async-done(((bf16[256,2048]{1,0:T(8,128)(2,1)}), bf16[1024,2048]{1,0:T(8,128)(2,1)}) %all-gather.2.cloned.1.call-update) | async-done | bytes 4194320 | tf_op jit(solution)/shard_map/all_gather | solution.py:209
  165.4 16.8 %attend.4 = (bf16[256,8192]{1,0:T(8,128)(2,1)}, bf16[256,8192]{1,0:T(8,128)(2,1)}, bf16[1024,512]{1,0:T(8,128)(2,1)}) custom-call(s32[8]{0:T(128)} %reshape.49.blocks_ref, s32[2]{0:T(128)} %bitcast.27, s32[1]{0:T(128)} %bitcast.1.base_ref, bf16[256,256]{1,0:T(8,128)(2,1)} %get-tuple-element.25.perm_ref, bf16[256,6272]{1,0:T(8,128)(2,1)} %bitcast.16, ...), custom_call_target="tpu_custom_call" | custom-call | flops 5368709120 | bytes 6291456 | tf_op jit(solution)/shard_map/attend/pallas_call | solution.py:252
  182.2 0.0 reduce-scatter.3.cloned.1.call-update
  182.2 2.8 prep_qg.3
  185.0 8.3 %all-to-all-done.1 = bf16[32,8,8192]{2,1,0:T(8,128)(2,1)} async-done(((bf16[32,8,8192]{2,1,0:T(8,128)(2,1)}), bf16[32,8,8192]{2,1,0:T(8,128)(2,1)}, u32[]{:S(2)}, u32[]{:S(2)}) %all-to-all-start.1) | async-done | bytes 4194336 | tf_op jit(solution)/shard_map/all_to_all | solution.py:172
  193.3 3.7 %all-to-all-start.3 = ((bf16[32,8,2048]{2,1,0:T(8,128)(2,1)}), bf16[32,8,2048]{2,1,0:T(8,128)(2,1)S(1)}, u32[]{:S(2)}, u32[]{:S(2)}) async-start(bf16[32,8,2048]{2,1,0:T(8,128)(2,1)} %bitcast.10), calls=%async_computation.4 | async-start | bytes 2097152 | tf_op jit(solution)/shard_map/all_to_all | solution.py:172
  197.1 0.2 reduce-scatter.5.cloned.1.call-start
  197.3 30.8 %attend.5 = (bf16[256,8192]{1,0:T(8,128)(2,1)}, bf16[256,8192]{1,0:T(8,128)(2,1)}, bf16[1024,1024]{1,0:T(8,128)(2,1)}) custom-call(s32[8]{0:T(128)} %reshape.49.blocks_ref, s32[2]{0:T(128)} %bitcast.28, s32[1]{0:T(128)} %bitcast.1.base_ref, bf16[256,256]{1,0:T(8,128)(2,1)} %get-tuple-element.25.perm_ref, ...), custom_call_target="tpu_custom_call", output_to_operand_aliasing={{0}: (7, {}), {1}: (8, {})} | custom-call | flops 10737418240 | bytes 12582912 | tf_op jit(solution)/shard_map/attend/pallas_call | solution.py:252
  228.1 0.0 reduce-scatter.3.cloned.1.call-done.refs_0_
  228.1 0.0 reduce-scatter.5.cloned.1.call-update
  228.1 0.0 all-to-all-done.3
  228.1 0.0 copy-start.2
  228.1 6.1 %all-to-all-start.2 = ((bf16[32,8,2048]{2,1,0:T(8,128)(2,1)}), bf16[32,8,2048]{2,1,0:T(8,128)(2,1)S(1)}, u32[]{:S(2)}, u32[]{:S(2)}) async-start(bf16[32,8,2048]{2,1,0:T(8,128)(2,1)} %bitcast.8), calls=%async_computation.3 | async-start | bytes 2097152 | tf_op jit(solution)/shard_map/all_to_all | solution.py:172
  234.2 0.0 copy-done.2
  234.2 10.0 %attend.6 = (bf16[256,8192]{1,0:T(8,128)(2,1)}, bf16[256,8192]{1,0:T(8,128)(2,1)}, bf16[1024,512]{1,0:T(8,128)(2,1)}) custom-call(s32[8]{0:T(128)} %reshape.49.blocks_ref, s32[2]{0:T(128)} %bitcast.29, s32[1]{0:T(128)} %bitcast.1.base_ref, bf16[256,256]{1,0:T(8,128)(2,1)} %get-tuple-element.25.perm_ref, ...), custom_call_target="tpu_custom_call", output_to_operand_aliasing={{0}: (7, {}), {1}: (8, {})} | custom-call | flops 2684354560 | bytes 3145728 | tf_op jit(solution)/shard_map/attend/pallas_call | solution.py:252
  244.2 16.0 %all-to-all-done.2 = bf16[32,8,2048]{2,1,0:T(8,128)(2,1)S(1)} async-done(((bf16[32,8,2048]{2,1,0:T(8,128)(2,1)}), bf16[32,8,2048]{2,1,0:T(8,128)(2,1)S(1)}, u32[]{:S(2)}, u32[]{:S(2)}) %all-to-all-start.2) | async-done | bytes 1048608 | tf_op jit(solution)/shard_map/all_to_all | solution.py:172
  260.2 0.0 copy-start.1
  260.2 1.0 copy-done.1
  261.2 10.0 %attend.7 = (bf16[256,8192]{1,0:T(8,128)(2,1)}, bf16[256,8192]{1,0:T(8,128)(2,1)}, bf16[1024,512]{1,0:T(8,128)(2,1)}) custom-call(s32[8]{0:T(128)} %reshape.49.blocks_ref, s32[2]{0:T(128)} %bitcast.30, s32[1]{0:T(128)} %bitcast.1.base_ref, bf16[256,256]{1,0:T(8,128)(2,1)} %get-tuple-element.25.perm_ref, ...), custom_call_target="tpu_custom_call", output_to_operand_aliasing={{0}: (7, {}), {1}: (8, {}), {2}: (9, {})} | custom-call | flops 2684354560 | bytes 3145728 | tf_op jit(solution)/shard_map/attend/pallas_call | solution.py:252
  271.1 18.8 %all_to_all.31 = bf16[4,256,512]{2,1,0:T(8,128)(2,1)} all-to-all(bf16[4,256,512]{2,1,0:T(8,128)(2,1)} %bitcast.19), channel_id=1, replica_groups=mesh['dp'=8,'ctx'=4] {'ctx'}, dimensions={0} | all-to-all | bytes 2097152 | tf_op jit(solution)/shard_map/all_to_all | solution.py:310
  289.9 0.0 reduce-scatter.5.cloned.1.call-done.refs_1_
  289.9 2.8 finish.1
Async XLA Ops:
  13.3 80.2 %all-to-all-start = ((bf16[32,8,6272]{2,1,0:T(8,128)(2,1)}), bf16[32,8,6272]{2,1,0:T(8,128)(2,1)S(1)}, u32[]{:S(2)}, u32[]{:S(2)}) async-start(bf16[32,8,6272]{2,1,0:T(8,128)(2,1)} %bitcast.17), calls=%async_computation | async-start | bytes 6422528 | tf_op jit(solution)/shard_map/all_to_all | solution.py:172
  93.5 1.7 copy-start
  95.1 98.2 %all-to-all-start.1 = ((bf16[32,8,8192]{2,1,0:T(8,128)(2,1)}), bf16[32,8,8192]{2,1,0:T(8,128)(2,1)}, u32[]{:S(2)}, u32[]{:S(2)}) async-start(bf16[32,8,8192]{2,1,0:T(8,128)(2,1)} %bitcast.14), calls=%async_computation.1 | async-start | bytes 8388608 | tf_op jit(solution)/shard_map/all_to_all | solution.py:172
  99.2 3.6 %copy-start.3 = (s32[1,2,4]{2,1,0:T(2,128)S(1)}, s32[1,2,4]{2,1,0:T(2,128)}, u32[]{:S(2)}) copy-start(s32[1,2,4]{2,1,0:T(2,128)} %param.12) | copy-start | bytes 100
  99.2 66.1 %all-gather.2.cloned.1.call-start = ((), (), s32[]{:S(2)}) async-start(), calls=%async_computation.7 | async-start | bytes 5242880 | tf_op jit(solution)/shard_map/all_gather | solution.py:209
  102.8 125.3 %reduce-scatter.3.cloned.1.call-start = ((), (), s32[]{:S(2)}) async-start(), calls=%async_computation.8 | async-start | bytes 1310720 | tf_op jit(solution)/shard_map/reduce_scatter | solution.py:298
  193.3 34.7 %all-to-all-start.3 = ((bf16[32,8,2048]{2,1,0:T(8,128)(2,1)}), bf16[32,8,2048]{2,1,0:T(8,128)(2,1)S(1)}, u32[]{:S(2)}, u32[]{:S(2)}) async-start(bf16[32,8,2048]{2,1,0:T(8,128)(2,1)} %bitcast.10), calls=%async_computation.4 | async-start | bytes 2097152 | tf_op jit(solution)/shard_map/all_to_all | solution.py:172
  197.1 92.8 %reduce-scatter.5.cloned.1.call-start = ((), (), s32[]{:S(2)}) async-start(), calls=%async_computation.9 | async-start | bytes 2621440 | tf_op jit(solution)/shard_map/reduce_scatter | solution.py:298
  228.1 6.1 %copy-start.2 = (bf16[32,8,2048]{2,1,0:T(8,128)(2,1)}, bf16[32,8,2048]{2,1,0:T(8,128)(2,1)S(1)}, u32[]{:S(2)}) copy-start(bf16[32,8,2048]{2,1,0:T(8,128)(2,1)S(1)} %all-to-all-done.3) | copy-start | bytes 3145732
  228.1 32.1 %all-to-all-start.2 = ((bf16[32,8,2048]{2,1,0:T(8,128)(2,1)}), bf16[32,8,2048]{2,1,0:T(8,128)(2,1)S(1)}, u32[]{:S(2)}, u32[]{:S(2)}) async-start(bf16[32,8,2048]{2,1,0:T(8,128)(2,1)} %bitcast.8), calls=%async_computation.3 | async-start | bytes 2097152 | tf_op jit(solution)/shard_map/all_to_all | solution.py:172
  260.2 1.0 copy-start.1
Sparse Core Ops, SparseCore 0:
  102.9 62.3 all-gather.1
  182.3 33.9 reduce-scatter.2
  228.2 35.4 reduce-scatter.4

commit v2 on v1

--- a/solution.py
+++ b/solution.py
@@ -21,7 +21,8 @@
 def chunk_sizes(heads):
     if heads < 4:
         return [1] * heads
-    return [heads // 4, heads - heads // 4 - TAIL, 1, 1]
+    half = (heads - TAIL) // 2
+    return [half, heads - TAIL - half, 1, 1]
 
 
 def dot(a, b, ca, cb):
@@ -63,8 +64,8 @@
     out_ref[:, width:] = dot(perm, grad_ref[...], 1, 0).astype(BF16)
 
 
-def place_kernel(recv_ref, out_ref, perm_ref):
-    rows, width = out_ref.shape
+def place_kernel(parts, kv_width, recv_ref, perm_ref, *out_refs):
+    rows = perm_ref.shape[0]
     end = recv_ref.shape[1] - HD
     slot = recv_ref[:, end : end + 1].astype(F32) + 128.0 * recv_ref[
         :, end + 1 : end + 2
@@ -72,7 +73,13 @@
     target = lax.broadcasted_iota(jnp.int32, (rows, rows), 1).astype(F32)
     perm = jnp.transpose((target == slot).astype(F32)).astype(BF16)
     perm_ref[...] = perm
-    out_ref[...] = dot(perm, recv_ref[:, end - width : end], 1, 0).astype(BF16)
+    at = end - 2 * kv_width
+    for part, out_ref in zip(parts, out_refs):
+        width = part * HD
+        out_ref[:, 0:width] = dot(perm, recv_ref[:, at : at + width], 1, 0).astype(BF16)
+        values = recv_ref[:, at + kv_width : at + kv_width + width]
+        out_ref[:, width:] = dot(perm, values, 1, 0).astype(BF16)
+        at += width
 
 
 def finish_kernel(sizes, *refs):
@@ -197,16 +204,15 @@
         name="prep_first",
     )(dest_col, dest_row, query_rows, grad_out, key_rows, value_rows)
     received = [exchange(sent)]
-    placed, perm = pl.pallas_call(
-        place_kernel,
-        out_shape=(
-            jax.ShapeDtypeStruct((rows, 2 * kv_width), BF16),
-            jax.ShapeDtypeStruct((rows, rows), BF16),
-        ),
+    parts = [p for p in (sizes[0], kv_heads - sizes[0]) if p]
+    perm, *placed = pl.pallas_call(
+        functools.partial(place_kernel, parts, kv_width),
+        out_shape=[jax.ShapeDtypeStruct((rows, rows), BF16)]
+        + [jax.ShapeDtypeStruct((rows, 2 * part * HD), BF16) for part in parts],
         compiler_params=params,
         name="place_kv",
     )(received[0])
-    kv_all = lax.all_gather(placed, "ctx", axis=0, tiled=True)
+    gathered = [lax.all_gather(x, "ctx", axis=0, tiled=True) for x in placed]
 
     def send(c):
         first, size = sum(sizes[:c]), sizes[c]
@@ -236,12 +242,16 @@
 
     def attend(c, recv, out, dq, dkv, dkv_heads, dkv_first):
         first, size = sum(sizes[:c]), sizes[c]
+        which = min(c, 1)
+        kv_all = gathered[which]
+        head = first - which * sizes[0]
+        value_head = parts[which] + head
         operands = [perm, recv, kv_all, kv_all]
         in_specs = [
             pl.BlockSpec((rows, rows), lambda j, *_: (0, 0)),
             pl.BlockSpec((rows, 2 * head_width), lambda j, *_: (0, j)),
-            pl.BlockSpec((seq, HD), lambda j, *_: (0, first + j)),
-            pl.BlockSpec((seq, HD), lambda j, *_: (0, kv_heads + first + j)),
+            pl.BlockSpec((seq, HD), lambda j, *_: (0, head + j)),
+            pl.BlockSpec((seq, HD), lambda j, *_: (0, value_head + j)),
         ]
         aliases = {}
         for place, array in enumerate((out, dq, dkv)):
@@ -292,7 +302,8 @@
             sent = send(c + 1)
             if c >= 1:
                 held = sums[: min(c - 1, tail_from)]
-                sent, dkv, held = lax.optimization_barrier((sent, dkv, held))
+                sent, dkv, held, last = lax.optimization_barrier((sent, dkv, held, gathered[-1]))
+                gathered[-1] = last
                 sums[: len(held)] = held
                 if c - 1 < tail_from:
                     sums[c - 1] = lax.psum_scatter(dkv, "ctx", scatter_dimension=0, tiled=True)

time: 300 us -> 306 us (1.020)
  blocking collectives: 18.8 us -> 123 us
  waiting for transfers between devices: 151 us -> 60.7 us
  starting transfers between devices: 21.5 us -> 12.9 us
    all_to_all x0 -> x1, blocking collectives: none -> 104 us  [exchange(): lax.all_to_all(x.reshape(peers, rows // peers, x.shape[1]), ('dp', 'ctx')...]
    all_to_all x4 -> x3, waiting for transfers between devices: 91.4 us -> 29.8 us  [exchange(): lax.all_to_all(x.reshape(peers, rows // peers, x.shape[1]), ('dp', 'ctx')...]
    all_gather x1 -> x2, waiting for transfers between devices: 59.1 us -> 30.1 us  [body(): gathered = [lax.all_gather(x, 'ctx', axis=0, tiled=True) for x in placed]]
    all_to_all x4 -> x3, starting transfers between devices: 21.2 us -> 12.6 us  [exchange(): lax.all_to_all(x.reshape(peers, rows // peers, x.shape[1]), ('dp', 'ctx')...]
  transfers between devices with their start and end apart: 7 -> 7, of which waited for: 4 -> 4; matrix products, arithmetic and copies ran while one was open for 0% -> 0% of each run, Pallas kernels for 28% -> 26%
where the time goes in v2:
time: 306 us
  blocking collectives  123 us (40%)
  Pallas kernels  90.5 us (30%)
  waiting for transfers between devices  60.7 us (20%)
  between operations  13.8 us (5%)
  starting transfers between devices  12.9 us (4%)
  local copies, waits for them, and re-layouts  4.79 us (2%)
    all_to_all x1, blocking collectives, exchange(): lax.all_to_all(x.reshape(peers, rows // peers, x.shape[1]), ('dp', 'ctx')...  104 us
    pallas_call x4, Pallas kernels, attend(): pl.pallas_call(functools.partial(attend_kernel, groups, slots), grid_spec...  67.4 us
    all_gather x2, waiting for transfers between devices, body(): gathered = [lax.all_gather(x, 'ctx', axis=0, tiled=True) for x in placed]  30.1 us
    all_to_all x3, waiting for transfers between devices, exchange(): lax.all_to_all(x.reshape(peers, rows // peers, x.shape[1]), ('dp', 'ctx')...  29.8 us
    all_to_all x1, blocking collectives, body(): lax.all_to_all(tail, 'ctx', split_axis=0, concat_axis=0, tiled=True)  18.8 us
    all_to_all x3, starting transfers between devices, exchange(): lax.all_to_all(x.reshape(peers, rows // peers, x.shape[1]), ('dp', 'ctx')...  12.6 us
    pallas_call x3, Pallas kernels, send(): pl.pallas_call(prep_qg_kernel, grid=(size,), in_specs=[pl.BlockSpec((rows...  10.9 us
  transfers between devices with their start and end apart: 7, of which 4 were waited for; matrix products, arithmetic and copies ran while one was open for 0% of the time, Pallas kernels for 26%

profile of v2, /device:TPU:0, one launch (start us, length us, event | category | flops | bytes accessed | tf_op | source)
XLA Modules:
  0.0 305.7 jit_solution(1379209332592082137)
XLA Ops:
  7.2 0.0 all-gather.3.cloned.1.call-start
  7.2 1.5 copy.18.col_ref
  8.7 5.6 %prep_first.1 = bf16[256,8320]{1,0:T(8,128)(2,1)} custom-call(s32[256,1]{1,0:T(8,128)} %copy.18.col_ref, s32[1,256]{1,0:T(1,128)} %bitcast.24, bf16[256,8192]{1,0:T(8,128)(2,1)} %query_ref.7, bf16[256,8192]{1,0:T(8,128)(2,1)} %grad_ref.7, bf16[256,1024]{1,0:T(8,128)(2,1)} %key_ref.1, bf16[256,1024]{1,0:T(8,128)(2,1)} %value_ref.1), custom_call_target="tpu_custom_call" | custom-call | tf_op jit(solution)/shard_map/prep_first/pallas_call | solution.py:190
  14.3 104.2 %all_to_all.31 = bf16[32,8,8320]{2,1,0:T(8,128)(2,1)} all-to-all(bf16[32,8,8320]{2,1,0:T(8,128)(2,1)} %bitcast.16), channel_id=1, replica_groups=mesh['dp'=8,'ctx'=4] {'dp','ctx'}, dimensions={0} | all-to-all | bytes 8519680 | tf_op jit(solution)/shard_map/all_to_all | solution.py:179
  118.5 3.8 %place_kv.1 = (bf16[256,256]{1,0:T(8,128)(2,1)}, bf16[256,768]{1,0:T(8,128)(2,1)}, bf16[256,1280]{1,0:T(8,128)(2,1)}) custom-call(bf16[256,8320]{1,0:T(8,128)(2,1)} %bitcast.14), custom_call_target="tpu_custom_call" | custom-call | tf_op jit(solution)/shard_map/place_kv/pallas_call | solution.py:208
  122.3 0.0 all-gather.3.cloned.1.call-update
  122.3 5.3 %prep_qg.4 = bf16[256,6144]{1,0:T(8,128)(2,1)} custom-call(s32[256,1]{1,0:T(8,128)} %copy.18.col_ref, s32[1,256]{1,0:T(1,128)} %bitcast.25, bf16[256,8192]{1,0:T(8,128)(2,1)} %query_ref.7, bf16[256,8192]{1,0:T(8,128)(2,1)} %grad_ref.7), custom_call_target="tpu_custom_call" | custom-call | flops 805306368 | bytes 6291456 | tf_op jit(solution)/shard_map/prep_qg/pallas_call | solution.py:219
  127.6 0.0 copy-start.3
  127.6 2.9 all-to-all-start.1
  130.5 0.0 all-gather.5.cloned.1.call-start
  130.6 0.7 all-gather.5.cloned.1.call-update
  131.3 0.0 reduce-scatter.3.cloned.1.call-start
  131.3 0.0 copy-done.3
  131.3 0.7 reshape.49.blocks_ref
  132.0 2.8 prep_qg.5
  134.8 20.2 %all-gather.3.cloned.1.call-done.key_ref.value_ref = bf16[1024,768]{1,0:T(8,128)(2,1)} async-done(((bf16[256,768]{1,0:T(8,128)(2,1)}), bf16[1024,768]{1,0:T(8,128)(2,1)}) %all-gather.3.cloned.1.call-update) | async-done | bytes 1572880 | tf_op jit(solution)/shard_map/all_gather | solution.py:215
  155.0 23.7 %attend.4 = (bf16[256,8192]{1,0:T(8,128)(2,1)}, bf16[256,8192]{1,0:T(8,128)(2,1)}, bf16[1024,768]{1,0:T(8,128)(2,1)}) custom-call(s32[8]{0:T(128)} %reshape.49.blocks_ref, s32[2]{0:T(128)} %bitcast.28, s32[1]{0:T(128)} %bitcast.1.base_ref, bf16[256,256]{1,0:T(8,128)(2,1)} %get-tuple-element.28.perm_ref, bf16[256,8320]{1,0:T(8,128)(2,1)} %bitcast.15, ...), custom_call_target="tpu_custom_call" | custom-call | flops 8053063680 | bytes 9437184 | tf_op jit(solution)/shard_map/attend/pallas_call | solution.py:262
  178.7 9.9 %all-gather.5.cloned.1.call-done.key_ref.value_ref = bf16[1024,1280]{1,0:T(8,128)(2,1)} async-done(((bf16[256,1280]{1,0:T(8,128)(2,1)}), bf16[1024,1280]{1,0:T(8,128)(2,1)}) %all-gather.5.cloned.1.call-update) | async-done | bytes 2621456 | tf_op jit(solution)/shard_map/all_gather | solution.py:215
  188.6 0.0 reduce-scatter.3.cloned.1.call-update
  188.7 13.7 %all-to-all-done.1 = bf16[32,8,6144]{2,1,0:T(8,128)(2,1)S(1)} async-done(((bf16[32,8,6144]{2,1,0:T(8,128)(2,1)}), bf16[32,8,6144]{2,1,0:T(8,128)(2,1)S(1)}, u32[]{:S(2)}, u32[]{:S(2)}) %all-to-all-start.1) | async-done | bytes 3145760 | tf_op jit(solution)/shard_map/all_to_all | solution.py:179
  202.4 0.0 copy-start.2
  202.4 1.6 copy-done.2
  204.0 3.6 %all-to-all-start.3 = ((bf16[32,8,2048]{2,1,0:T(8,128)(2,1)}), bf16[32,8,2048]{2,1,0:T(8,128)(2,1)S(1)}, u32[]{:S(2)}, u32[]{:S(2)}) async-start(bf16[32,8,2048]{2,1,0:T(8,128)(2,1)} %bitcast.10), calls=%async_computation.4 | async-start | bytes 2097152 | tf_op jit(solution)/shard_map/all_to_all | solution.py:179
  207.7 0.2 reduce-scatter.5.cloned.1.call-start
  207.9 2.8 prep_qg.3
  210.7 23.8 %attend.5 = (bf16[256,8192]{1,0:T(8,128)(2,1)}, bf16[256,8192]{1,0:T(8,128)(2,1)}, bf16[1024,768]{1,0:T(8,128)(2,1)}) custom-call(s32[8]{0:T(128)} %reshape.49.blocks_ref, s32[2]{0:T(128)} %bitcast.29, s32[1]{0:T(128)} %bitcast.1.base_ref, bf16[256,256]{1,0:T(8,128)(2,1)} %get-tuple-element.28.perm_ref, ...), custom_call_target="tpu_custom_call", output_to_operand_aliasing={{0}: (7, {}), {1}: (8, {})} | custom-call | flops 8053063680 | bytes 9437184 | tf_op jit(solution)/shard_map/attend/pallas_call | solution.py:262
  234.5 0.0 reduce-scatter.3.cloned.1.call-done.refs_0_
  234.5 0.0 reduce-scatter.5.cloned.1.call-update
  234.6 0.0 all-to-all-done.3
  234.6 0.0 copy-start
  234.6 6.1 %all-to-all-start.2 = ((bf16[32,8,2048]{2,1,0:T(8,128)(2,1)}), bf16[32,8,2048]{2,1,0:T(8,128)(2,1)S(1)}, u32[]{:S(2)}, u32[]{:S(2)}) async-start(bf16[32,8,2048]{2,1,0:T(8,128)(2,1)} %bitcast.8), calls=%async_computation.3 | async-start | bytes 2097152 | tf_op jit(solution)/shard_map/all_to_all | solution.py:179
  240.7 0.0 copy-done
  240.7 9.9 %attend.6 = (bf16[256,8192]{1,0:T(8,128)(2,1)}, bf16[256,8192]{1,0:T(8,128)(2,1)}, bf16[1024,512]{1,0:T(8,128)(2,1)}) custom-call(s32[8]{0:T(128)} %reshape.49.blocks_ref, s32[2]{0:T(128)} %bitcast.30, s32[1]{0:T(128)} %bitcast.1.base_ref, bf16[256,256]{1,0:T(8,128)(2,1)} %get-tuple-element.28.perm_ref, ...), custom_call_target="tpu_custom_call", output_to_operand_aliasing={{0}: (7, {}), {1}: (8, {})} | custom-call | flops 2684354560 | bytes 3145728 | tf_op jit(solution)/shard_map/attend/pallas_call | solution.py:262
  250.6 16.1 %all-to-all-done.2 = bf16[32,8,2048]{2,1,0:T(8,128)(2,1)S(1)} async-done(((bf16[32,8,2048]{2,1,0:T(8,128)(2,1)}), bf16[32,8,2048]{2,1,0:T(8,128)(2,1)S(1)}, u32[]{:S(2)}, u32[]{:S(2)}) %all-to-all-start.2) | async-done | bytes 1048608 | tf_op jit(solution)/shard_map/all_to_all | solution.py:179
  266.7 0.0 copy-start.1
  266.7 1.0 copy-done.1
  267.7 9.9 %attend.7 = (bf16[256,8192]{1,0:T(8,128)(2,1)}, bf16[256,8192]{1,0:T(8,128)(2,1)}, bf16[1024,512]{1,0:T(8,128)(2,1)}) custom-call(s32[8]{0:T(128)} %reshape.49.blocks_ref, s32[2]{0:T(128)} %bitcast.31, s32[1]{0:T(128)} %bitcast.1.base_ref, bf16[256,256]{1,0:T(8,128)(2,1)} %get-tuple-element.28.perm_ref, ...), custom_call_target="tpu_custom_call", output_to_operand_aliasing={{0}: (7, {}), {1}: (8, {}), {2}: (9, {})} | custom-call | flops 2684354560 | bytes 3145728 | tf_op jit(solution)/shard_map/attend/pallas_call | solution.py:262
  277.6 18.8 %all_to_all.32 = bf16[4,256,512]{2,1,0:T(8,128)(2,1)} all-to-all(bf16[4,256,512]{2,1,0:T(8,128)(2,1)} %bitcast.20), channel_id=1, replica_groups=mesh['dp'=8,'ctx'=4] {'ctx'}, dimensions={0} | all-to-all | bytes 2097152 | tf_op jit(solution)/shard_map/all_to_all | solution.py:321
  296.4 0.0 reduce-scatter.5.cloned.1.call-done.refs_1_
  296.4 2.8 finish.1
Async XLA Ops:
  7.2 147.8 %all-gather.3.cloned.1.call-start = ((), (), s32[]{:S(2)}) async-start(), calls=%async_computation.7 | async-start | bytes 1966080 | tf_op jit(solution)/shard_map/all_gather | solution.py:215
  127.6 3.7 %copy-start.3 = (s32[1,2,4]{2,1,0:T(2,128)S(1)}, s32[1,2,4]{2,1,0:T(2,128)}, u32[]{:S(2)}) copy-start(s32[1,2,4]{2,1,0:T(2,128)} %param.12) | copy-start | bytes 100
  127.6 74.8 %all-to-all-start.1 = ((bf16[32,8,6144]{2,1,0:T(8,128)(2,1)}), bf16[32,8,6144]{2,1,0:T(8,128)(2,1)S(1)}, u32[]{:S(2)}, u32[]{:S(2)}) async-start(bf16[32,8,6144]{2,1,0:T(8,128)(2,1)} %bitcast.17), calls=%async_computation.1 | async-start | bytes 6291456 | tf_op jit(solution)/shard_map/all_to_all | solution.py:179
  130.5 58.1 %all-gather.5.cloned.1.call-start = ((), (), s32[]{:S(2)}) async-start(), calls=%async_computation.8 | async-start | bytes 3276800 | tf_op jit(solution)/shard_map/all_gather | solution.py:215
  131.3 103.3 %reduce-scatter.3.cloned.1.call-start = ((), (), s32[]{:S(2)}) async-start(), calls=%async_computation.9 | async-start | bytes 1966080 | tf_op jit(solution)/shard_map/reduce_scatter | solution.py:309
  202.4 1.6 copy-start.2
  204.0 30.5 %all-to-all-start.3 = ((bf16[32,8,2048]{2,1,0:T(8,128)(2,1)}), bf16[32,8,2048]{2,1,0:T(8,128)(2,1)S(1)}, u32[]{:S(2)}, u32[]{:S(2)}) async-start(bf16[32,8,2048]{2,1,0:T(8,128)(2,1)} %bitcast.10), calls=%async_computation.4 | async-start | bytes 2097152 | tf_op jit(solution)/shard_map/all_to_all | solution.py:179
  207.7 88.7 %reduce-scatter.5.cloned.1.call-start = ((), (), s32[]{:S(2)}) async-start(), calls=%async_computation.10 | async-start | bytes 1966080 | tf_op jit(solution)/shard_map/reduce_scatter | solution.py:309
  234.6 6.1 %copy-start = (bf16[32,8,2048]{2,1,0:T(8,128)(2,1)}, bf16[32,8,2048]{2,1,0:T(8,128)(2,1)S(1)}, u32[]{:S(2)}) copy-start(bf16[32,8,2048]{2,1,0:T(8,128)(2,1)S(1)} %all-to-all-done.3) | copy-start | bytes 3145732
  234.6 32.1 %all-to-all-start.2 = ((bf16[32,8,2048]{2,1,0:T(8,128)(2,1)}), bf16[32,8,2048]{2,1,0:T(8,128)(2,1)S(1)}, u32[]{:S(2)}, u32[]{:S(2)}) async-start(bf16[32,8,2048]{2,1,0:T(8,128)(2,1)} %bitcast.8), calls=%async_computation.3 | async-start | bytes 2097152 | tf_op jit(solution)/shard_map/all_to_all | solution.py:179
  266.7 1.0 copy-start.1
Sparse Core Ops, SparseCore 0:
  122.4 32.5 all-gather.2
  156.6 32.0 all-gather.4
  191.2 39.4 reduce-scatter.2
  234.7 32.3 reduce-scatter.4
